TPU v7x, 32 devices: a whole 2x2x4 slice. The times are simulated.
32 devices in a mesh: ifg: 4 (over x, core), rows: 8 (over z, y).
Axes of the slice: x: 2, y: 2, z: 4, core: 2. Of those that a mesh axis runs over, the one named last changes fastest.
Arguments:
- phase: bfloat16 [512, 64, 512], P('ifg', 'rows')
- coherence: bfloat16 [512, 64, 512], P('ifg', 'rows'), may hold values from 0.0996 to 0.95
- height: float32 [64, 512], P('rows')
- gap_mask: int32 [512, 64], P('ifg', 'rows'), may hold values 0 or 1
- date_pairs: int32 [512, 2], replicated, may hold values from 0 to 299, as said below
Outputs:
- displacement: float32 [300, 64, 512], P(None, 'rows', 'ifg')
- topo_slope: float32 [512], P('ifg')
Inputs may be any that keep to these rules, and one draw needn't show every extreme that they name: date_pairs[i, 0] < date_pairs[i, 1] for every interferogram.
All inputs are finite; a program needn't handle non-finite values. No bound on the sum of `gap_mask` on one device may be relied on, other than what follows from the above.
Results may differ from a plain program's by a relative error of at most 0.0028.
Values may be sent and summed in bfloat16 or wider, within the bound.
A program may use at most 128 MiB of HBM per device.

v0:
```python
import functools

import jax
import jax.numpy as jnp
from jax import lax
from jax.experimental import pallas as pl
from jax.experimental.pallas import tpu as pltpu
from jax.sharding import PartitionSpec as P

DATES = 300
DPAD = 304
KPAD = 384
LANES = 128
CHUNK = 16
SMOOTHING_WEIGHT = 0.5
RIDGE_WEIGHT = 0.05
F32 = jnp.float32
BF16 = jnp.bfloat16
MESH = pl.DeviceIdType.MESH


def split(value):
    high = value.astype(BF16)
    low = (value - high.astype(F32)).astype(BF16)
    return high, low


def dot(a, b):
    return jnp.dot(a, b, preferred_element_type=F32)


def kernel(
    n, m,
    phase, coher, height, gap, pairs,
    out, topo_out,
    ph_s, co_s, edge, halo, sm_s, w_send, w_all, c_send, c_all,
    mom, mom_all, topo_s, g, gt, vb,
    r_s, w_s, n_s, p_s, s_s, z_s,
    pack, halo_row, halo_col, red_a, red_b,
    halo_sems, w_sems, c_sems, own_sems, mom_sems, row_sems, col_sems, a_sems, b_sems,
):
    count, rows, width = phase.shape
    ifgs = pairs.shape[1]
    tiles = width // LANES
    chunks = count // CHUNK
    me = lax.axis_index("ifg")
    my_row = lax.axis_index("rows")
    has_up, has_down = my_row > 0, my_row < m - 1
    has_left, has_right = me > 0, me < n - 1

    barrier = pltpu.get_barrier_semaphore()
    for k in range(1, n):
        pl.semaphore_signal(barrier, inc=1, device_id=(lax.rem(me + k, n), my_row), device_id_type=MESH)
    for k in range(1, m):
        pl.semaphore_signal(barrier, inc=1, device_id=(me, lax.rem(my_row + k, m)), device_id_type=MESH)

    def remote(src, dst, sems, index, target):
        return pltpu.make_async_remote_copy(
            src_ref=src, dst_ref=dst,
            send_sem=sems.at[(0,) + index], recv_sem=sems.at[(1,) + index],
            device_id=target, device_id_type=MESH,
        )

    def widen(c, _):
        for src, dst in ((phase, ph_s), (coher, co_s)):
            block = src[pl.ds(c * CHUNK, CHUNK)].astype(F32).reshape(CHUNK * rows, width)
            for t in range(tiles):
                dst[t, pl.ds(pl.multiple_of(c * CHUNK * rows, CHUNK * rows), CHUNK * rows), :] = (
                    block[:, t * LANES:(t + 1) * LANES]
                )
        return 0

    lax.fori_loop(0, chunks, widen, 0)

    def row_of(ref, j, i0, size):
        return jnp.concatenate(
            [ref[t, pl.ds(i0 * rows + j, size, stride=rows), :] for t in range(tiles)], axis=1
        )

    def take_edges(c, _):
        i0 = pl.multiple_of(c * CHUNK, CHUNK)
        for side, j in ((0, 0), (1, rows - 1)):
            for a, ref in ((0, ph_s), (1, co_s)):
                edge[side, a, pl.ds(i0, CHUNK), :] = row_of(ref, j, i0, CHUNK).astype(BF16)
        return 0

    lax.fori_loop(0, chunks, take_edges, 0)

    pl.semaphore_wait(barrier, n + m - 2)

    send_up = remote(edge.at[0], halo.at[1], halo_sems, (0,), (me, lax.max(my_row - 1, 0)))
    send_down = remote(edge.at[1], halo.at[0], halo_sems, (1,), (me, lax.min(my_row + 1, m - 1)))

    @pl.when(has_up)
    def _():
        send_up.start()

    @pl.when(has_down)
    def _():
        send_down.start()

    mom[...] = jnp.zeros_like(mom)
    lane = lax.broadcasted_iota(jnp.int32, (CHUNK, width), 1)

    def box(vert):
        before = jnp.where(lane == 0, 0.0, pltpu.roll(vert, 1, 1))
        after = jnp.where(lane == width - 1, 0.0, pltpu.roll(vert, width - 1, 1))
        return vert + before + after

    def smooth_rows(low, high):
        def body(c, _):
            i0 = pl.multiple_of(c * CHUNK, CHUNK)
            gaps = gap[pl.ds(i0, CHUNK), :].astype(F32)

            def load(j):
                if j < 0 or j == rows:
                    side = 0 if j < 0 else 1
                    ph = halo[side, 0, pl.ds(i0, CHUNK), :].astype(F32)
                    co = halo[side, 1, pl.ds(i0, CHUNK), :].astype(F32)
                else:
                    ph = row_of(ph_s, j, i0, CHUNK)
                    co = row_of(co_s, j, i0, CHUNK)
                return ph * co, co

            window = [load(low - 1), load(low)]
            top_sum = jnp.zeros((CHUNK, LANES), F32)
            low_sum = jnp.zeros((CHUNK, LANES), F32)
            for j in range(low, high):
                window.append(load(j + 1))
                numer = box(window[0][0] + window[1][0] + window[2][0])
                denom = box(window[0][1] + window[1][1] + window[2][1])
                window.pop(0)
                smooth = numer / denom
                mean = denom * (1.0 / 9.0)
                weight = (gaps[:, j:j + 1] * mean).astype(BF16)
                for d in range(n):
                    w_send[d, j, pl.ds(i0, CHUNK), :] = weight[:, d * LANES:(d + 1) * LANES]
                sm_s[j, pl.ds(i0, CHUNK), :] = smooth
                terrain = height[j:j + 1, :]
                scaled = mean * terrain
                top = scaled * smooth
                low_part = scaled * terrain
                for t in range(tiles):
                    top_sum += top[:, t * LANES:(t + 1) * LANES]
                    low_sum += low_part[:, t * LANES:(t + 1) * LANES]
            mom[0, pl.ds(i0, CHUNK), :] += top_sum
            mom[1, pl.ds(i0, CHUNK), :] += low_sum
            return 0

        lax.fori_loop(0, chunks, body, 0)

    mine = pl.ds(pl.multiple_of(me * count, count), count)

    def exchange(src, dst, sems, part, low, high):
        span = pl.ds(low, high - low)
        copies = []
        for k in range(n - 1, 0, -1):
            d = lax.rem(me + k, n)
            copy = remote(src.at[d, span], dst.at[span, mine, :], sems, (part, k), (d, my_row))
            copy.start()
            copies.append(copy)
        own = pltpu.make_async_copy(src.at[me, span], dst.at[span, mine, :], sems.at[0, part, 0])
        own.start()
        copies.append(own)
        return copies

    half = rows // 2
    pending = []
    smooth_rows(1, half)
    pending += exchange(w_send, w_all, w_sems, 0, 1, half)
    smooth_rows(half, rows - 1)
    pending += exchange(w_send, w_all, w_sems, 1, half, rows - 1)

    date = lax.broadcasted_iota(jnp.int32, (KPAD, ifgs), 0)
    signs = (date == pairs[1:2, :]).astype(F32) - (date == pairs[0:1, :]).astype(F32)
    gt[...] = signs[:DPAD].astype(BF16)
    g[...] = signs.T.astype(BF16)
    vb[...] = jnp.zeros_like(vb)

    @pl.when(has_up)
    def _():
        send_up.wait_send()
        send_down.wait_recv()

    @pl.when(jnp.logical_not(has_up))
    def _():
        halo[0] = jnp.zeros_like(halo[0])

    @pl.when(has_down)
    def _():
        send_down.wait_send()
        send_up.wait_recv()

    @pl.when(jnp.logical_not(has_down))
    def _():
        halo[1] = jnp.zeros_like(halo[1])

    smooth_rows(0, 1)
    smooth_rows(rows - 1, rows)

    top_row = jnp.sum(mom[0].T, axis=0, keepdims=True)
    low_row = jnp.sum(mom[1].T, axis=0, keepdims=True)
    mom_all[my_row] = jnp.concatenate([top_row, low_row, jnp.zeros((6, LANES), F32)], axis=0)
    mom_copies = []
    for k in range(1, m):
        copy = remote(mom_all.at[my_row], mom_all.at[my_row], mom_sems, (k,), (me, lax.rem(my_row + k, m)))
        copy.start()
        mom_copies.append(copy)
    pending += exchange(w_send, w_all, w_sems, 2, 0, 1)
    pending += exchange(w_send, w_all, w_sems, 3, rows - 1, rows)
    for copy in mom_copies:
        copy.wait()
    sums = mom_all[0]
    for k in range(1, m):
        sums = sums + mom_all[k]
    slope = sums[0:1, :] / sums[1:2, :]
    topo_out[...] = slope[:, :count]
    topo_s[...] = jnp.broadcast_to(slope, (LANES, LANES)).T

    def correct_rows(low, high):
        def body(c, _):
            i0 = pl.multiple_of(c * CHUNK, CHUNK)
            column = topo_s[pl.ds(i0, CHUNK), :]
            for j in range(low, high):
                for d in range(n):
                    cols = pl.ds(d * LANES, LANES)
                    value = sm_s[j, pl.ds(i0, CHUNK), cols] - column * height[j:j + 1, cols]
                    c_send[d, j, pl.ds(i0, CHUNK), :] = value.astype(BF16)
            return 0

        lax.fori_loop(0, chunks, body, 0)

    correct_rows(0, half)
    first = exchange(c_send, c_all, c_sems, 0, 0, half)
    correct_rows(half, rows)
    second = exchange(c_send, c_all, c_sems, 1, half, rows)

    def back_project(u):
        high, low = split(u)
        return dot(gt[...], high) + dot(gt[...], low)

    def right_rows(q, _):
        u = jnp.concatenate(
            [w_all[2 * q + i].astype(F32) * c_all[2 * q + i].astype(F32) for i in range(2)], axis=1
        )
        b = back_project(u)
        for i in range(2):
            r_s[2 * q + i] = b[:, i * LANES:(i + 1) * LANES]
        return 0

    for copy in pending:
        copy.wait()
    for copy in first:
        copy.wait()
    lax.fori_loop(0, half // 2, right_rows, 0)
    for copy in second:
        copy.wait()
    lax.fori_loop(half // 2, half, right_rows, 0)

    small = lax.broadcasted_iota(jnp.int32, (DPAD, LANES), 1)

    def start_halo(v, step):
        first_packed = jnp.zeros((DPAD, LANES), F32)
        last_packed = jnp.zeros((DPAD, LANES), F32)
        for j in range(rows):
            tile = v[j]
            first_packed = jnp.where(small == j, pltpu.roll(tile, j, 1) if j else tile, first_packed)
            last_packed = jnp.where(small == j, pltpu.roll(tile, j + 1, 1), last_packed)
        pack[step, 0] = first_packed
        pack[step, 1] = last_packed
        copies = (
            (has_up, remote(v.at[0], halo_row.at[step, 1], row_sems, (step, 0), (me, lax.max(my_row - 1, 0)))),
            (has_down, remote(v.at[rows - 1], halo_row.at[step, 0], row_sems, (step, 1), (me, lax.min(my_row + 1, m - 1)))),
            (has_left, remote(pack.at[step, 0], halo_col.at[step, 1], col_sems, (step, 0), (lax.max(me - 1, 0), my_row))),
            (has_right, remote(pack.at[step, 1], halo_col.at[step, 0], col_sems, (step, 1), (lax.min(me + 1, n - 1), my_row))),
        )
        for there, copy in copies:
            pl.when(there)(copy.start)
        return copies

    def wait_halo(copies, step):
        for there, copy in copies:
            pl.when(there)(copy.wait_send)
        for index, buffer in ((0, halo_row), (1, halo_col)):
            low_there, low_copy = copies[2 * index]
            high_there, high_copy = copies[2 * index + 1]
            for side, there, copy in ((0, low_there, high_copy), (1, high_there, low_copy)):
                pl.when(there)(copy.wait_recv)

                @pl.when(jnp.logical_not(there))
                def _(side=side, buffer=buffer):
                    buffer[step, side] = jnp.zeros((DPAD, LANES), F32)

    def apply(v, target, step, middle):
        copies = start_halo(v, step)

        def body(q, _):
            high, low = split(jnp.concatenate([v[2 * q], v[2 * q + 1]], axis=1))
            vb[0, :DPAD, :] = high
            vb[1, :DPAD, :] = low
            diff = dot(g[...], vb[0]) + dot(g[...], vb[1])
            u = jnp.concatenate(
                [diff[:, i * LANES:(i + 1) * LANES] * w_all[2 * q + i].astype(F32) for i in range(2)], axis=1
            )
            image = back_project(u)
            for i in range(2):
                target[2 * q + i] = image[:, i * LANES:(i + 1) * LANES]
            return 0

        lax.fori_loop(0, half // 2, body, 0)
        middle()
        lax.fori_loop(half // 2, half, body, 0)
        wait_halo(copies, step)
        left_col, right_col = halo_col[step, 0], halo_col[step, 1]
        for j in range(rows):
            here = v[j]
            above = v[j - 1] if j else halo_row[step, 0]
            below = v[j + 1] if j < rows - 1 else halo_row[step, 1]
            left_edge = pltpu.roll(left_col, LANES - j, 1) if j else left_col
            right_edge = pltpu.roll(right_col, LANES - 1 - j, 1)
            left = jnp.where(small == 0, left_edge, pltpu.roll(here, 1, 1))
            right = jnp.where(small == LANES - 1, right_edge, pltpu.roll(here, LANES - 1, 1))
            spread = 4.0 * here - (above + below + left + right)
            target[j] = target[j] + SMOOTHING_WEIGHT * spread + RIDGE_WEIGHT * here

    def fold(value):
        return jnp.sum(value, axis=0, keepdims=True)

    def reduce_first(step, parts):
        filled = list(parts) + [jnp.zeros((8 - len(parts), LANES), F32)]
        red_a[step, me] = jnp.concatenate(filled, axis=0)
        copies = []
        for k in range(1, n):
            copy = remote(red_a.at[step, me], red_a.at[step, me], a_sems, (step, k), (lax.rem(me + k, n), my_row))
            copy.start()
            copies.append(copy)
        return copies

    def reduce_second(step, copies):
        for copy in copies:
            copy.wait()
        total = red_a[step, 0]
        for k in range(1, n):
            total = total + red_a[step, k]
        red_b[step, my_row] = total
        later = []
        for k in range(1, m):
            copy = remote(red_b.at[step, my_row], red_b.at[step, my_row], b_sems, (step, k), (me, lax.rem(my_row + k, m)))
            copy.start()
            later.append(copy)
        return later

    def reduce_last(step, copies):
        for copy in copies:
            copy.wait()
        total = red_b[step, 0]
        for k in range(1, m):
            total = total + red_b[step, k]
        total = jnp.sum(total, axis=1, keepdims=True)
        return [total[i:i + 1, :] for i in range(3)]

    def overlapped(step, parts, v, target, apply_step):
        state = {"copies": reduce_first(step, parts)}

        def middle():
            state["copies"] = reduce_second(step, state["copies"])

        apply(v, target, apply_step, middle)
        return reduce_last(step, state["copies"])

    apply(r_s, w_s, 0, lambda: None)
    gamma_sum = jnp.zeros((1, LANES), F32)
    delta_sum = jnp.zeros((1, LANES), F32)
    for j in range(rows):
        gamma_sum += fold(r_s[j] * r_s[j])
        delta_sum += fold(r_s[j] * w_s[j])
    gamma, curve, _ = overlapped(0, (gamma_sum, delta_sum), w_s, n_s, 1)

    alpha = gamma / curve
    alpha_first = alpha
    gamma_sum = jnp.zeros((1, LANES), F32)
    delta_sum = jnp.zeros((1, LANES), F32)
    cross_sum = jnp.zeros((1, LANES), F32)
    for j in range(rows):
        p, s, z = r_s[j], w_s[j], n_s[j]
        r = p - alpha * s
        w = s - alpha * z
        p_s[j], s_s[j], z_s[j] = p, s, z
        r_s[j], w_s[j] = r, w
        gamma_sum += fold(r * r)
        delta_sum += fold(r * w)
        cross_sum += fold(r * s)
    gamma_next, delta, cross = overlapped(1, (gamma_sum, delta_sum, cross_sum), w_s, n_s, 2)

    beta = gamma_next / gamma
    gamma = gamma_next
    curve = delta + 2.0 * beta * cross + beta * beta * curve
    alpha = gamma / curve
    gamma_sum = jnp.zeros((1, LANES), F32)
    delta_sum = jnp.zeros((1, LANES), F32)
    cross_sum = jnp.zeros((1, LANES), F32)
    for j in range(rows):
        r, w = r_s[j], w_s[j]
        first_p = p_s[j]
        p = r + beta * first_p
        s = w + beta * s_s[j]
        z = n_s[j] + beta * z_s[j]
        r = r - alpha * s
        w = w - alpha * z
        p_s[j] = p
        r_s[j] = r
        z_s[j] = alpha_first * first_p + alpha * p
        gamma_sum += fold(r * r)
        delta_sum += fold(r * w)
        cross_sum += fold(r * s)
    copies = reduce_first(2, (gamma_sum, delta_sum, cross_sum))
    gamma_next, delta, cross = reduce_last(2, reduce_second(2, copies))
    beta = gamma_next / gamma
    curve = delta + 2.0 * beta * cross + beta * beta * curve
    alpha = gamma_next / curve
    for j in range(rows):
        x = z_s[j] + alpha * (r_s[j] + beta * p_s[j])
        out[pl.ds(j, DATES, stride=rows), :] = x[:DATES]


def solution(mesh):
    n, m = mesh.shape["ifg"], mesh.shape["rows"]

    def per_device(phase, coherence, height, gap_mask, date_pairs):
        count, rows, width = phase.shape
        ifgs = date_pairs.shape[0]
        tiles = width // LANES
        dma = pltpu.SemaphoreType.DMA
        state = pltpu.VMEM((rows, DPAD, LANES), F32)
        vmem = pl.BlockSpec(memory_space=pltpu.VMEM)
        displacement, topo = pl.pallas_call(
            functools.partial(kernel, n, m),
            out_shape=(
                jax.ShapeDtypeStruct((DATES * rows, LANES), F32),
                jax.ShapeDtypeStruct((1, count), F32),
            ),
            in_specs=[vmem] * 5,
            out_specs=(vmem, vmem),
            scratch_shapes=[
                pltpu.VMEM((tiles, count * rows, LANES), F32),
                pltpu.VMEM((tiles, count * rows, LANES), F32),
                pltpu.VMEM((2, 2, count, width), BF16),
                pltpu.VMEM((2, 2, count, width), BF16),
                pltpu.VMEM((rows, count, width), F32),
                pltpu.VMEM((n, rows, count, LANES), BF16),
                pltpu.VMEM((rows, ifgs, LANES), BF16),
                pltpu.VMEM((n, rows, count, LANES), BF16),
                pltpu.VMEM((rows, ifgs, LANES), BF16),
                pltpu.VMEM((2, LANES, LANES), F32),
                pltpu.VMEM((m, 8, LANES), F32),
                pltpu.VMEM((LANES, LANES), F32),
                pltpu.VMEM((ifgs, KPAD), BF16),
                pltpu.VMEM((DPAD, ifgs), BF16),
                pltpu.VMEM((2, KPAD, 2 * LANES), BF16),
                state, state, state, state, state, state,
                pltpu.VMEM((3, 2, DPAD, LANES), F32),
                pltpu.VMEM((3, 2, DPAD, LANES), F32),
                pltpu.VMEM((3, 2, DPAD, LANES), F32),
                pltpu.VMEM((3, n, 8, LANES), F32),
                pltpu.VMEM((3, m, 8, LANES), F32),
                dma((2, 2)),
                dma((2, 4, n)),
                dma((2, 2, n)),
                dma((1,)),
                dma((2, m)),
                dma((2, 3, 2)),
                dma((2, 3, 2)),
                dma((2, 3, n)),
                dma((2, 3, m)),
            ],
            compiler_params=pltpu.CompilerParams(
                collective_id=0, has_side_effects=True, vmem_limit_bytes=56 * 1024 * 1024
            ),
        )(phase, coherence, height, gap_mask, date_pairs.T)
        return displacement.reshape(DATES, rows, LANES), topo.reshape(count)

    return jax.shard_map(
        per_device,
        mesh=mesh,
        in_specs=(
            P("ifg", "rows", None),
            P("ifg", "rows", None),
            P("rows", None),
            P("ifg", "rows"),
            P(),
        ),
        out_specs=(P(None, "rows", "ifg"), P("ifg")),
        check_vma=False,
    )
```

profile of v0, /device:TPU:0, one launch (start us, length us, event | category | flops | bytes accessed | tf_op | source)
XLA Modules:
  0.0 84.6 jit_solution(4053142123372947268)
XLA Ops:
  0.6 1.4 %copy.7.gap = s32[128,8]{1,0:T(8,128)} copy(s32[128,8]{0,1:T(8,128)} %param.8) | data formatting | bytes 8192 | tf_op args[3]
  2.0 79.6 %shard_map.68 = (f32[2400,128]{1,0:T(8,128)}, f32[1,128]{1,0:T(1,128)}) custom-call(bf16[128,8,512]{2,1,0:T(8,128)(2,1)} %phase.1, bf16[128,8,512]{2,1,0:T(8,128)(2,1)} %coher.1, f32[8,512]{1,0:T(8,128)} %height.1, s32[128,8]{1,0:T(8,128)} %copy.7.gap, s32[2,512]{1,0:T(2,128)} %bitcast.4), custom_call_target="tpu_custom_call" | custom-call | tf_op jit(solution)/shard_map/pallas_call | solution.py:436
  81.7 0.0 copy-start
  81.7 2.4 %copy.10 = f32[300,8,128]{2,1,0:T(8,128)} copy(f32[300,8,128]{2,1,0:T(8,128)} %bitcast.3) | data formatting | bytes 2457600
  84.1 0.0 copy-done
  84.1 0.5 copy.11
Async XLA Ops:
  81.7 2.4 %copy-start = (f32[1,128]{1,0:T(1,128)S(1)}, f32[1,128]{1,0:T(1,128)}, u32[]{:S(2)}) copy-start(f32[1,128]{1,0:T(1,128)} %get-tuple-element.5) | copy-start | bytes 1540
where the time goes:
time: 84.8 us; the launch traced here: 84.6 us
  Pallas kernels  79.6 us (94%)
  local copies, waits for them, and re-layouts  4.33 us (5%)
    pallas_call x1, Pallas kernels, per_device(): pl.pallas_call(functools.partial(kernel, n, m), out_shape=(jax.ShapeDtype...  79.6 us
    unnamed x5, local copies, waits for them, and re-layouts  4.33 us

commit v1 on v0

--- a/solution.py
+++ b/solution.py
@@ -34,10 +34,10 @@
     phase, coher, height, gap, pairs,
     out, topo_out,
     ph_s, co_s, edge, halo, sm_s, w_send, w_all, c_send, c_all,
-    mom, mom_all, topo_s, g, gt, vb,
+    h_halo, gap_s, mom, mom_all, topo_s, g, gt, vb,
     r_s, w_s, n_s, p_s, s_s, z_s,
     pack, halo_row, halo_col, red_a, red_b,
-    halo_sems, w_sems, c_sems, own_sems, mom_sems, row_sems, col_sems, a_sems, b_sems,
+    h_sems, halo_sems, w_sems, c_sems, mom_sems, row_sems, col_sems, a_sems, b_sems,
 ):
     count, rows, width = phase.shape
     ifgs = pairs.shape[1]
@@ -77,6 +77,29 @@
             [ref[t, pl.ds(i0 * rows + j, size, stride=rows), :] for t in range(tiles)], axis=1
         )
 
+    gap_s[...] = gap[...].astype(F32).T
+    pl.semaphore_wait(barrier, n + m - 2)
+    up, down = (me, lax.max(my_row - 1, 0)), (me, lax.min(my_row + 1, m - 1))
+
+    def start_pair(sent_up, sent_down, landing, sems):
+        to_up = remote(sent_up, landing.at[1], sems, (0,), up)
+        to_down = remote(sent_down, landing.at[0], sems, (1,), down)
+        pl.when(has_up)(to_up.start)
+        pl.when(has_down)(to_down.start)
+        return to_up, to_down
+
+    def wait_pair(copies, landing):
+        to_up, to_down = copies
+        for there, sent, received, side in ((has_up, to_up, to_down, 0), (has_down, to_down, to_up, 1)):
+            pl.when(there)(sent.wait_send)
+            pl.when(there)(received.wait_recv)
+
+            @pl.when(jnp.logical_not(there))
+            def _(side=side):
+                landing[side] = jnp.zeros_like(landing[side])
+
+    terrain_copies = start_pair(height, height, h_halo, h_sems)
+
     def take_edges(c, _):
         i0 = pl.multiple_of(c * CHUNK, CHUNK)
         for side, j in ((0, 0), (1, rows - 1)):
@@ -84,25 +107,9 @@
                 edge[side, a, pl.ds(i0, CHUNK), :] = row_of(ref, j, i0, CHUNK).astype(BF16)
         return 0
 
-    lax.fori_loop(0, chunks, take_edges, 0)
-
-    pl.semaphore_wait(barrier, n + m - 2)
-
-    send_up = remote(edge.at[0], halo.at[1], halo_sems, (0,), (me, lax.max(my_row - 1, 0)))
-    send_down = remote(edge.at[1], halo.at[0], halo_sems, (1,), (me, lax.min(my_row + 1, m - 1)))
-
-    @pl.when(has_up)
-    def _():
-        send_up.start()
-
-    @pl.when(has_down)
-    def _():
-        send_down.start()
-
-    mom[...] = jnp.zeros_like(mom)
-    lane = lax.broadcasted_iota(jnp.int32, (CHUNK, width), 1)
 
     def box(vert):
+        lane = lax.broadcasted_iota(jnp.int32, vert.shape, 1)
         before = jnp.where(lane == 0, 0.0, pltpu.roll(vert, 1, 1))
         after = jnp.where(lane == width - 1, 0.0, pltpu.roll(vert, width - 1, 1))
         return vert + before + after
@@ -110,7 +117,7 @@
     def smooth_rows(low, high):
         def body(c, _):
             i0 = pl.multiple_of(c * CHUNK, CHUNK)
-            gaps = gap[pl.ds(i0, CHUNK), :].astype(F32)
+            gaps = gap_s[pl.ds(i0, CHUNK), :]
 
             def load(j):
                 if j < 0 or j == rows:
@@ -123,8 +130,6 @@
                 return ph * co, co
 
             window = [load(low - 1), load(low)]
-            top_sum = jnp.zeros((CHUNK, LANES), F32)
-            low_sum = jnp.zeros((CHUNK, LANES), F32)
             for j in range(low, high):
                 window.append(load(j + 1))
                 numer = box(window[0][0] + window[1][0] + window[2][0])
@@ -136,15 +141,6 @@
                 for d in range(n):
                     w_send[d, j, pl.ds(i0, CHUNK), :] = weight[:, d * LANES:(d + 1) * LANES]
                 sm_s[j, pl.ds(i0, CHUNK), :] = smooth
-                terrain = height[j:j + 1, :]
-                scaled = mean * terrain
-                top = scaled * smooth
-                low_part = scaled * terrain
-                for t in range(tiles):
-                    top_sum += top[:, t * LANES:(t + 1) * LANES]
-                    low_sum += low_part[:, t * LANES:(t + 1) * LANES]
-            mom[0, pl.ds(i0, CHUNK), :] += top_sum
-            mom[1, pl.ds(i0, CHUNK), :] += low_sum
             return 0
 
         lax.fori_loop(0, chunks, body, 0)
@@ -168,6 +164,52 @@
     pending = []
     smooth_rows(1, half)
     pending += exchange(w_send, w_all, w_sems, 0, 1, half)
+
+    wait_pair(terrain_copies, h_halo)
+
+    def box_terrain(take):
+        here = take(height[...])
+        above = take(h_halo[0])[rows - 1:]
+        below = take(h_halo[1])[:1]
+        vert = here + jnp.concatenate([above, here[:-1]], axis=0) + jnp.concatenate([here[1:], below], axis=0)
+        return box(vert)
+
+    terrain_box = box_terrain(lambda h: h)
+    square_box = box_terrain(lambda h: h * h)
+
+    def moments(c, _):
+        start = pl.multiple_of(c * CHUNK * rows, CHUNK * rows)
+        top = jnp.zeros((CHUNK, rows, LANES), F32)
+        low = jnp.zeros((CHUNK, rows, LANES), F32)
+        for t in range(tiles):
+            cols = slice(t * LANES, (t + 1) * LANES)
+            co = co_s[t, pl.ds(start, CHUNK * rows), :].reshape(CHUNK, rows, LANES)
+            ph = ph_s[t, pl.ds(start, CHUNK * rows), :].reshape(CHUNK, rows, LANES)
+            top += co * ph * terrain_box[None, :, cols]
+            low += co * square_box[None, :, cols]
+        mom[0, pl.ds(start, CHUNK * rows), :] = top.reshape(CHUNK * rows, LANES)
+        mom[1, pl.ds(start, CHUNK * rows), :] = low.reshape(CHUNK * rows, LANES)
+        return 0
+
+    lax.fori_loop(0, chunks, moments, 0)
+
+    def summed(index):
+        total = mom[index, pl.ds(0, count, stride=rows), :]
+        for j in range(1, rows):
+            total += mom[index, pl.ds(j, count, stride=rows), :]
+        if count < LANES:
+            total = jnp.concatenate([total, jnp.zeros((LANES - count, LANES), F32)], axis=0)
+        return jnp.sum(total.T, axis=0, keepdims=True)
+
+    mom_all[my_row] = jnp.concatenate([summed(0), summed(1), jnp.zeros((6, LANES), F32)], axis=0)
+    mom_copies = []
+    for k in range(1, m):
+        copy = remote(mom_all.at[my_row], mom_all.at[my_row], mom_sems, (k,), (me, lax.rem(my_row + k, m)))
+        copy.start()
+        mom_copies.append(copy)
+
+    lax.fori_loop(0, chunks, take_edges, 0)
+    edge_copies = start_pair(edge.at[0], edge.at[1], halo, halo_sems)
     smooth_rows(half, rows - 1)
     pending += exchange(w_send, w_all, w_sems, 1, half, rows - 1)
 
@@ -177,37 +219,6 @@
     g[...] = signs.T.astype(BF16)
     vb[...] = jnp.zeros_like(vb)
 
-    @pl.when(has_up)
-    def _():
-        send_up.wait_send()
-        send_down.wait_recv()
-
-    @pl.when(jnp.logical_not(has_up))
-    def _():
-        halo[0] = jnp.zeros_like(halo[0])
-
-    @pl.when(has_down)
-    def _():
-        send_down.wait_send()
-        send_up.wait_recv()
-
-    @pl.when(jnp.logical_not(has_down))
-    def _():
-        halo[1] = jnp.zeros_like(halo[1])
-
-    smooth_rows(0, 1)
-    smooth_rows(rows - 1, rows)
-
-    top_row = jnp.sum(mom[0].T, axis=0, keepdims=True)
-    low_row = jnp.sum(mom[1].T, axis=0, keepdims=True)
-    mom_all[my_row] = jnp.concatenate([top_row, low_row, jnp.zeros((6, LANES), F32)], axis=0)
-    mom_copies = []
-    for k in range(1, m):
-        copy = remote(mom_all.at[my_row], mom_all.at[my_row], mom_sems, (k,), (me, lax.rem(my_row + k, m)))
-        copy.start()
-        mom_copies.append(copy)
-    pending += exchange(w_send, w_all, w_sems, 2, 0, 1)
-    pending += exchange(w_send, w_all, w_sems, 3, rows - 1, rows)
     for copy in mom_copies:
         copy.wait()
     sums = mom_all[0]
@@ -230,10 +241,17 @@
 
         lax.fori_loop(0, chunks, body, 0)
 
-    correct_rows(0, half)
-    first = exchange(c_send, c_all, c_sems, 0, 0, half)
-    correct_rows(half, rows)
-    second = exchange(c_send, c_all, c_sems, 1, half, rows)
+    correct_rows(1, half)
+    pending += exchange(c_send, c_all, c_sems, 0, 1, half)
+    correct_rows(half, rows - 1)
+    pending += exchange(c_send, c_all, c_sems, 1, half, rows - 1)
+    wait_pair(edge_copies, halo)
+    last = []
+    for part, j in ((2, 0), (3, rows - 1)):
+        smooth_rows(j, j + 1)
+        last += exchange(w_send, w_all, w_sems, part, j, j + 1)
+        correct_rows(j, j + 1)
+        last += exchange(c_send, c_all, c_sems, part, j, j + 1)
 
     def back_project(u):
         high, low = split(u)
@@ -250,12 +268,11 @@
 
     for copy in pending:
         copy.wait()
-    for copy in first:
+    lax.fori_loop(1, half - 1, right_rows, 0)
+    for copy in last:
         copy.wait()
-    lax.fori_loop(0, half // 2, right_rows, 0)
-    for copy in second:
-        copy.wait()
-    lax.fori_loop(half // 2, half, right_rows, 0)
+    right_rows(0, 0)
+    right_rows(half - 1, 0)
 
     small = lax.broadcasted_iota(jnp.int32, (DPAD, LANES), 1)
 
@@ -266,13 +283,16 @@
             tile = v[j]
             first_packed = jnp.where(small == j, pltpu.roll(tile, j, 1) if j else tile, first_packed)
             last_packed = jnp.where(small == j, pltpu.roll(tile, j + 1, 1), last_packed)
-        pack[step, 0] = first_packed
-        pack[step, 1] = last_packed
+        pack[step, 0] = v[0].astype(BF16)
+        pack[step, 1] = v[rows - 1].astype(BF16)
+        pack[step, 2] = first_packed.astype(BF16)
+        pack[step, 3] = last_packed.astype(BF16)
+        left, right = (lax.max(me - 1, 0), my_row), (lax.min(me + 1, n - 1), my_row)
         copies = (
-            (has_up, remote(v.at[0], halo_row.at[step, 1], row_sems, (step, 0), (me, lax.max(my_row - 1, 0)))),
-            (has_down, remote(v.at[rows - 1], halo_row.at[step, 0], row_sems, (step, 1), (me, lax.min(my_row + 1, m - 1)))),
-            (has_left, remote(pack.at[step, 0], halo_col.at[step, 1], col_sems, (step, 0), (lax.max(me - 1, 0), my_row))),
-            (has_right, remote(pack.at[step, 1], halo_col.at[step, 0], col_sems, (step, 1), (lax.min(me + 1, n - 1), my_row))),
+            (has_up, remote(pack.at[step, 0], halo_row.at[step, 1], row_sems, (step, 0), up)),
+            (has_down, remote(pack.at[step, 1], halo_row.at[step, 0], row_sems, (step, 1), down)),
+            (has_left, remote(pack.at[step, 2], halo_col.at[step, 1], col_sems, (step, 0), left)),
+            (has_right, remote(pack.at[step, 3], halo_col.at[step, 0], col_sems, (step, 1), right)),
         )
         for there, copy in copies:
             pl.when(there)(copy.start)
@@ -289,7 +309,7 @@
 
                 @pl.when(jnp.logical_not(there))
                 def _(side=side, buffer=buffer):
-                    buffer[step, side] = jnp.zeros((DPAD, LANES), F32)
+                    buffer[step, side] = jnp.zeros((DPAD, LANES), BF16)
 
     def apply(v, target, step, middle):
         copies = start_halo(v, step)
@@ -310,18 +330,27 @@
         lax.fori_loop(0, half // 2, body, 0)
         middle()
         lax.fori_loop(half // 2, half, body, 0)
-        wait_halo(copies, step)
-        left_col, right_col = halo_col[step, 0], halo_col[step, 1]
         for j in range(rows):
             here = v[j]
-            above = v[j - 1] if j else halo_row[step, 0]
-            below = v[j + 1] if j < rows - 1 else halo_row[step, 1]
+            around = jnp.where(small == 0, 0.0, pltpu.roll(here, 1, 1))
+            around += jnp.where(small == LANES - 1, 0.0, pltpu.roll(here, LANES - 1, 1))
+            if j:
+                around += v[j - 1]
+            if j < rows - 1:
+                around += v[j + 1]
+            spread = 4.0 * here - around
+            target[j] = target[j] + SMOOTHING_WEIGHT * spread + RIDGE_WEIGHT * here
+        wait_halo(copies, step)
+        left_col, right_col = halo_col[step, 0].astype(F32), halo_col[step, 1].astype(F32)
+        for j in range(rows):
             left_edge = pltpu.roll(left_col, LANES - j, 1) if j else left_col
             right_edge = pltpu.roll(right_col, LANES - 1 - j, 1)
-            left = jnp.where(small == 0, left_edge, pltpu.roll(here, 1, 1))
-            right = jnp.where(small == LANES - 1, right_edge, pltpu.roll(here, LANES - 1, 1))
-            spread = 4.0 * here - (above + below + left + right)
-            target[j] = target[j] + SMOOTHING_WEIGHT * spread + RIDGE_WEIGHT * here
+            beside = jnp.where(small == 0, left_edge, jnp.where(small == LANES - 1, right_edge, 0.0))
+            if j == 0:
+                beside += halo_row[step, 0].astype(F32)
+            if j == rows - 1:
+                beside += halo_row[step, 1].astype(F32)
+            target[j] = target[j] - SMOOTHING_WEIGHT * beside
 
     def fold(value):
         return jnp.sum(value, axis=0, keepdims=True)
@@ -451,22 +480,24 @@
                 pltpu.VMEM((rows, ifgs, LANES), BF16),
                 pltpu.VMEM((n, rows, count, LANES), BF16),
                 pltpu.VMEM((rows, ifgs, LANES), BF16),
-                pltpu.VMEM((2, LANES, LANES), F32),
+                pltpu.VMEM((2, rows, width), F32),
+                pltpu.VMEM((count, rows), F32),
+                pltpu.VMEM((2, count * rows, LANES), F32),
                 pltpu.VMEM((m, 8, LANES), F32),
                 pltpu.VMEM((LANES, LANES), F32),
                 pltpu.VMEM((ifgs, KPAD), BF16),
                 pltpu.VMEM((DPAD, ifgs), BF16),
                 pltpu.VMEM((2, KPAD, 2 * LANES), BF16),
                 state, state, state, state, state, state,
-                pltpu.VMEM((3, 2, DPAD, LANES), F32),
-                pltpu.VMEM((3, 2, DPAD, LANES), F32),
-                pltpu.VMEM((3, 2, DPAD, LANES), F32),
+                pltpu.VMEM((3, 4, DPAD, LANES), BF16),
+                pltpu.VMEM((3, 2, DPAD, LANES), BF16),
+                pltpu.VMEM((3, 2, DPAD, LANES), BF16),
                 pltpu.VMEM((3, n, 8, LANES), F32),
                 pltpu.VMEM((3, m, 8, LANES), F32),
                 dma((2, 2)),
+                dma((2, 2)),
                 dma((2, 4, n)),
-                dma((2, 2, n)),
-                dma((1,)),
+                dma((2, 4, n)),
                 dma((2, m)),
                 dma((2, 3, 2)),
                 dma((2, 3, 2)),
@@ -476,7 +507,7 @@
             compiler_params=pltpu.CompilerParams(
                 collective_id=0, has_side_effects=True, vmem_limit_bytes=56 * 1024 * 1024
             ),
-        )(phase, coherence, height, gap_mask, date_pairs.T)
+        )(phase, coherence, height, gap_mask.T, date_pairs.T)
         return displacement.reshape(DATES, rows, LANES), topo.reshape(count)
 
     return jax.shard_map(

time: 84.8 us -> 68.2 us (0.80)
  Pallas kernels: 79.6 us -> 64.4 us
  local copies, waits for them, and re-layouts: 4.33 us -> 2.91 us
    pallas_call x1, Pallas kernels: 79.6 us -> 64.4 us  [per_device(): pl.pallas_call(functools.partial(kernel, n, m), out_shape=(jax.ShapeDtype...]
    unnamed x5 -> x4, local copies, waits for them, and re-layouts: 4.33 us -> 2.91 us
where the time goes in v1:
time: 68.2 us; the launch traced here: 68 us
  Pallas kernels  64.4 us (94%)
  local copies, waits for them, and re-layouts  2.91 us (4%)
    pallas_call x1, Pallas kernels, per_device(): pl.pallas_call(functools.partial(kernel, n, m), out_shape=(jax.ShapeDtype...  64.4 us
    unnamed x4, local copies, waits for them, and re-layouts  2.91 us

profile of v1, /device:TPU:0, one launch (start us, length us, event | category | flops | bytes accessed | tf_op | source)
XLA Modules:
  0.0 68.0 jit_solution(2167404951787565443)
XLA Ops:
  0.6 64.4 %shard_map.68 = (f32[2400,128]{1,0:T(8,128)}, f32[1,128]{1,0:T(1,128)}) custom-call(bf16[128,8,512]{2,1,0:T(8,128)(2,1)} %phase.1, bf16[128,8,512]{2,1,0:T(8,128)(2,1)} %coher.1, f32[8,512]{1,0:T(8,128)} %height.1, s32[8,128]{1,0:T(8,128)} %bitcast.5, s32[2,512]{1,0:T(2,128)} %bitcast.6), custom_call_target="tpu_custom_call" | custom-call | tf_op jit(solution)/shard_map/pallas_call | solution.py:465
  65.1 0.0 copy-start
  65.1 2.4 %copy.9 = f32[300,8,128]{2,1,0:T(8,128)} copy(f32[300,8,128]{2,1,0:T(8,128)} %bitcast.4) | data formatting | bytes 2457600
  67.5 0.0 copy-done
  67.5 0.5 copy.10
Async XLA Ops:
  65.1 2.4 %copy-start = (f32[1,128]{1,0:T(1,128)S(1)}, f32[1,128]{1,0:T(1,128)}, u32[]{:S(2)}) copy-start(f32[1,128]{1,0:T(1,128)} %get-tuple-element.5) | copy-start | bytes 1540

commit v2 on v1

--- a/solution.py
+++ b/solution.py
@@ -9,9 +9,10 @@
 
 DATES = 300
 DPAD = 304
-KPAD = 384
+KPAD = 640
 LANES = 128
 CHUNK = 16
+BLOCK = 104
 SMOOTHING_WEIGHT = 0.5
 RIDGE_WEIGHT = 0.05
 F32 = jnp.float32
@@ -32,9 +33,9 @@
 def kernel(
     n, m,
     phase, coher, height, gap, pairs,
-    out, topo_out,
+    x_out, topo_out,
     ph_s, co_s, edge, halo, sm_s, w_send, w_all, c_send, c_all,
-    h_halo, gap_s, mom, mom_all, topo_s, g, gt, vb,
+    h_halo, gap_s, mom, mom_all, topo_s, g, gt,
     r_s, w_s, n_s, p_s, s_s, z_s,
     pack, halo_row, halo_col, red_a, red_b,
     h_sems, halo_sems, w_sems, c_sems, mom_sems, row_sems, col_sems, a_sems, b_sems,
@@ -161,9 +162,8 @@
         return copies
 
     half = rows // 2
-    pending = []
-    smooth_rows(1, half)
-    pending += exchange(w_send, w_all, w_sems, 0, 1, half)
+    smooth_rows(1, 3)
+    w_copies = [exchange(w_send, w_all, w_sems, 0, 1, 3)]
 
     wait_pair(terrain_copies, h_halo)
 
@@ -210,14 +210,16 @@
 
     lax.fori_loop(0, chunks, take_edges, 0)
     edge_copies = start_pair(edge.at[0], edge.at[1], halo, halo_sems)
-    smooth_rows(half, rows - 1)
-    pending += exchange(w_send, w_all, w_sems, 1, half, rows - 1)
+    for q in range(1, half - 1):
+        smooth_rows(2 * q + 1, 2 * q + 3)
+        w_copies.append(exchange(w_send, w_all, w_sems, q, 2 * q + 1, 2 * q + 3))
 
     date = lax.broadcasted_iota(jnp.int32, (KPAD, ifgs), 0)
+    date = jnp.where(date >= DPAD, date - DPAD, date)
     signs = (date == pairs[1:2, :]).astype(F32) - (date == pairs[0:1, :]).astype(F32)
-    gt[...] = signs[:DPAD].astype(BF16)
+    gt[:, :ifgs] = signs[:DPAD].astype(BF16)
+    gt[:, ifgs:] = signs[:DPAD].astype(BF16)
     g[...] = signs.T.astype(BF16)
-    vb[...] = jnp.zeros_like(vb)
 
     for copy in mom_copies:
         copy.wait()
@@ -241,38 +243,39 @@
 
         lax.fori_loop(0, chunks, body, 0)
 
-    correct_rows(1, half)
-    pending += exchange(c_send, c_all, c_sems, 0, 1, half)
-    correct_rows(half, rows - 1)
-    pending += exchange(c_send, c_all, c_sems, 1, half, rows - 1)
+    c_copies = []
+    for q in range(half - 1):
+        correct_rows(2 * q + 1, 2 * q + 3)
+        c_copies.append(exchange(c_send, c_all, c_sems, q, 2 * q + 1, 2 * q + 3))
     wait_pair(edge_copies, halo)
     last = []
-    for part, j in ((2, 0), (3, rows - 1)):
+    for part, j in ((half - 1, rows - 1), (half, 0)):
         smooth_rows(j, j + 1)
         last += exchange(w_send, w_all, w_sems, part, j, j + 1)
         correct_rows(j, j + 1)
         last += exchange(c_send, c_all, c_sems, part, j, j + 1)
 
+    def pair(q):
+        return 2 * q + 1, (2 * q + 2) % rows
+
+    def both(q, of):
+        return jnp.concatenate([of(j) for j in pair(q)], axis=1)
+
+    def put(target, q, value):
+        for i, j in enumerate(pair(q)):
+            target[j] = value[:, i * LANES:(i + 1) * LANES]
+
     def back_project(u):
-        high, low = split(u)
-        return dot(gt[...], high) + dot(gt[...], low)
-
-    def right_rows(q, _):
-        u = jnp.concatenate(
-            [w_all[2 * q + i].astype(F32) * c_all[2 * q + i].astype(F32) for i in range(2)], axis=1
-        )
-        b = back_project(u)
-        for i in range(2):
-            r_s[2 * q + i] = b[:, i * LANES:(i + 1) * LANES]
-        return 0
-
-    for copy in pending:
-        copy.wait()
-    lax.fori_loop(1, half - 1, right_rows, 0)
-    for copy in last:
-        copy.wait()
-    right_rows(0, 0)
-    right_rows(half - 1, 0)
+        return dot(gt[...], jnp.concatenate(split(u), axis=0))
+
+    def right_rows(q):
+        put(r_s, q, back_project(both(q, lambda j: w_all[j].astype(F32) * c_all[j].astype(F32))))
+
+    def weighted(v, target, q):
+        high, low = split(both(q, lambda j: v[j]))
+        filler = jnp.zeros((KPAD - 2 * DPAD, 2 * LANES), BF16)
+        diff = dot(g[...], jnp.concatenate([high, low, filler], axis=0))
+        put(target, q, back_project(diff * both(q, lambda j: w_all[j].astype(F32))))
 
     small = lax.broadcasted_iota(jnp.int32, (DPAD, LANES), 1)
 
@@ -311,25 +314,7 @@
                 def _(side=side, buffer=buffer):
                     buffer[step, side] = jnp.zeros((DPAD, LANES), BF16)
 
-    def apply(v, target, step, middle):
-        copies = start_halo(v, step)
-
-        def body(q, _):
-            high, low = split(jnp.concatenate([v[2 * q], v[2 * q + 1]], axis=1))
-            vb[0, :DPAD, :] = high
-            vb[1, :DPAD, :] = low
-            diff = dot(g[...], vb[0]) + dot(g[...], vb[1])
-            u = jnp.concatenate(
-                [diff[:, i * LANES:(i + 1) * LANES] * w_all[2 * q + i].astype(F32) for i in range(2)], axis=1
-            )
-            image = back_project(u)
-            for i in range(2):
-                target[2 * q + i] = image[:, i * LANES:(i + 1) * LANES]
-            return 0
-
-        lax.fori_loop(0, half // 2, body, 0)
-        middle()
-        lax.fori_loop(half // 2, half, body, 0)
+    def spread_and_halo(v, target, step, copies):
         for j in range(rows):
             here = v[j]
             around = jnp.where(small == 0, 0.0, pltpu.roll(here, 1, 1))
@@ -352,6 +337,14 @@
                 beside += halo_row[step, 1].astype(F32)
             target[j] = target[j] - SMOOTHING_WEIGHT * beside
 
+    def apply(v, target, step, middle):
+        copies = start_halo(v, step)
+        for q in range(half):
+            weighted(v, target, q)
+            if q == half // 2 - 1:
+                middle()
+        spread_and_halo(v, target, step, copies)
+
     def fold(value):
         return jnp.sum(value, axis=0, keepdims=True)
 
@@ -397,7 +390,17 @@
         apply(v, target, apply_step, middle)
         return reduce_last(step, state["copies"])
 
-    apply(r_s, w_s, 0, lambda: None)
+    for q in range(half - 1):
+        for copy in w_copies[q] + c_copies[q]:
+            copy.wait()
+        right_rows(q)
+        weighted(r_s, w_s, q)
+    for copy in last:
+        copy.wait()
+    right_rows(half - 1)
+    copies = start_halo(r_s, 0)
+    weighted(r_s, w_s, half - 1)
+    spread_and_halo(r_s, w_s, 0, copies)
     gamma_sum = jnp.zeros((1, LANES), F32)
     delta_sum = jnp.zeros((1, LANES), F32)
     for j in range(rows):
@@ -448,8 +451,14 @@
     curve = delta + 2.0 * beta * cross + beta * beta * curve
     alpha = gamma_next / curve
     for j in range(rows):
-        x = z_s[j] + alpha * (r_s[j] + beta * p_s[j])
-        out[pl.ds(j, DATES, stride=rows), :] = x[:DATES]
+        x_out[j] = z_s[j] + alpha * (r_s[j] + beta * p_s[j])
+
+
+def order_dates(x, topo, out, topo_out):
+    rows, dates, _ = x.shape
+    for j in range(rows):
+        out[pl.ds(j, dates, stride=rows), :] = x[j]
+    topo_out[...] = topo[...]
 
 
 def solution(mesh):
@@ -462,10 +471,10 @@
         dma = pltpu.SemaphoreType.DMA
         state = pltpu.VMEM((rows, DPAD, LANES), F32)
         vmem = pl.BlockSpec(memory_space=pltpu.VMEM)
-        displacement, topo = pl.pallas_call(
+        field, topo = pl.pallas_call(
             functools.partial(kernel, n, m),
             out_shape=(
-                jax.ShapeDtypeStruct((DATES * rows, LANES), F32),
+                jax.ShapeDtypeStruct((rows, DPAD, LANES), F32),
                 jax.ShapeDtypeStruct((1, count), F32),
             ),
             in_specs=[vmem] * 5,
@@ -486,8 +495,7 @@
                 pltpu.VMEM((m, 8, LANES), F32),
                 pltpu.VMEM((LANES, LANES), F32),
                 pltpu.VMEM((ifgs, KPAD), BF16),
-                pltpu.VMEM((DPAD, ifgs), BF16),
-                pltpu.VMEM((2, KPAD, 2 * LANES), BF16),
+                pltpu.VMEM((DPAD, 2 * ifgs), BF16),
                 state, state, state, state, state, state,
                 pltpu.VMEM((3, 4, DPAD, LANES), BF16),
                 pltpu.VMEM((3, 2, DPAD, LANES), BF16),
@@ -496,8 +504,8 @@
                 pltpu.VMEM((3, m, 8, LANES), F32),
                 dma((2, 2)),
                 dma((2, 2)),
-                dma((2, 4, n)),
-                dma((2, 4, n)),
+                dma((2, rows // 2 + 1, n)),
+                dma((2, rows // 2 + 1, n)),
                 dma((2, m)),
                 dma((2, 3, 2)),
                 dma((2, 3, 2)),
@@ -508,6 +516,22 @@
                 collective_id=0, has_side_effects=True, vmem_limit_bytes=56 * 1024 * 1024
             ),
         )(phase, coherence, height, gap_mask.T, date_pairs.T)
+        displacement, topo = pl.pallas_call(
+            order_dates,
+            grid=(pl.cdiv(DATES, BLOCK),),
+            out_shape=(
+                jax.ShapeDtypeStruct((DATES * rows, LANES), F32),
+                jax.ShapeDtypeStruct((1, count), F32),
+            ),
+            in_specs=[
+                pl.BlockSpec((rows, BLOCK, LANES), lambda i: (0, i, 0)),
+                pl.BlockSpec((1, count), lambda i: (0, 0)),
+            ],
+            out_specs=(
+                pl.BlockSpec((BLOCK * rows, LANES), lambda i: (i, 0)),
+                pl.BlockSpec((1, count), lambda i: (0, 0)),
+            ),
+        )(field, topo)
         return displacement.reshape(DATES, rows, LANES), topo.reshape(count)
 
     return jax.shard_map(

time: 68.2 us -> 67.4 us (0.988)
  local copies, waits for them, and re-layouts: 2.91 us -> 0 us
  Pallas kernels: 64.4 us -> 66.6 us
    pallas_call x0 -> x1, Pallas kernels: none -> 3.32 us  [per_device(): pl.pallas_call(order_dates, grid=(pl.cdiv(DATES, BLOCK),), out_shape=(jax...]
    unnamed x4 -> x0, local copies, waits for them, and re-layouts: 2.91 us -> none
    pallas_call x1, Pallas kernels: 64.4 us -> 63.3 us  [per_device(): pl.pallas_call(functools.partial(kernel, n, m), out_shape=(jax.ShapeDtype...]
where the time goes in v2:
time: 67.4 us; the launch traced here: 67.2 us
  Pallas kernels  66.6 us (99%)
    pallas_call x1, Pallas kernels, per_device(): pl.pallas_call(functools.partial(kernel, n, m), out_shape=(jax.ShapeDtype...  63.3 us
    pallas_call x1, Pallas kernels, per_device(): pl.pallas_call(order_dates, grid=(pl.cdiv(DATES, BLOCK),), out_shape=(jax...  3.32 us

profile of v2, /device:TPU:0, one launch (start us, length us, event | category | flops | bytes accessed | tf_op | source)
XLA Modules:
  0.0 67.2 jit_solution(17892702233210409041)
XLA Ops:
  0.6 63.3 %shard_map.68 = (f32[8,304,128]{2,1,0:T(8,128)}, f32[1,128]{1,0:T(1,128)}) custom-call(bf16[128,8,512]{2,1,0:T(8,128)(2,1)} %phase.1, bf16[128,8,512]{2,1,0:T(8,128)(2,1)} %coher.1, f32[8,512]{1,0:T(8,128)} %height.1, s32[8,128]{1,0:T(8,128)} %bitcast.4, s32[2,512]{1,0:T(2,128)} %bitcast.5), custom_call_target="tpu_custom_call" | custom-call | tf_op jit(solution)/shard_map/pallas_call | solution.py:474
  63.9 3.3 %shard_map.69 = (f32[2400,128]{1,0:T(8,128)}, f32[1,128]{1,0:T(1,128)}) custom-call(f32[8,304,128]{2,1,0:T(8,128)} %get-tuple-element.6.x, f32[1,128]{1,0:T(1,128)} %get-tuple-element.7.topo), custom_call_target="tpu_custom_call" | custom-call | tf_op jit(solution)/shard_map/pallas_call | solution.py:519

commit v3 on v2

--- a/solution.py
+++ b/solution.py
@@ -34,13 +34,13 @@
     n, m,
     phase, coher, height, gap, pairs,
     x_out, topo_out,
-    ph_s, co_s, edge, halo, sm_s, w_send, w_all, c_send, c_all,
-    h_halo, gap_s, mom, mom_all, topo_s, g, gt,
+    halo, sm_s, w_send, w_all, c_send, c_all,
+    h_halo, gap_s, mom, mom_all, topo_s, g, gt, pick, place,
     r_s, w_s, n_s, p_s, s_s, z_s,
     pack, halo_row, halo_col, red_a, red_b,
     h_sems, halo_sems, w_sems, c_sems, mom_sems, row_sems, col_sems, a_sems, b_sems,
 ):
-    count, rows, width = phase.shape
+    rows, count, width = phase.shape
     ifgs = pairs.shape[1]
     tiles = width // LANES
     chunks = count // CHUNK
@@ -62,22 +62,6 @@
             device_id=target, device_id_type=MESH,
         )
 
-    def widen(c, _):
-        for src, dst in ((phase, ph_s), (coher, co_s)):
-            block = src[pl.ds(c * CHUNK, CHUNK)].astype(F32).reshape(CHUNK * rows, width)
-            for t in range(tiles):
-                dst[t, pl.ds(pl.multiple_of(c * CHUNK * rows, CHUNK * rows), CHUNK * rows), :] = (
-                    block[:, t * LANES:(t + 1) * LANES]
-                )
-        return 0
-
-    lax.fori_loop(0, chunks, widen, 0)
-
-    def row_of(ref, j, i0, size):
-        return jnp.concatenate(
-            [ref[t, pl.ds(i0 * rows + j, size, stride=rows), :] for t in range(tiles)], axis=1
-        )
-
     gap_s[...] = gap[...].astype(F32).T
     pl.semaphore_wait(barrier, n + m - 2)
     up, down = (me, lax.max(my_row - 1, 0)), (me, lax.min(my_row + 1, m - 1))
@@ -101,14 +85,6 @@
 
     terrain_copies = start_pair(height, height, h_halo, h_sems)
 
-    def take_edges(c, _):
-        i0 = pl.multiple_of(c * CHUNK, CHUNK)
-        for side, j in ((0, 0), (1, rows - 1)):
-            for a, ref in ((0, ph_s), (1, co_s)):
-                edge[side, a, pl.ds(i0, CHUNK), :] = row_of(ref, j, i0, CHUNK).astype(BF16)
-        return 0
-
-
     def box(vert):
         lane = lax.broadcasted_iota(jnp.int32, vert.shape, 1)
         before = jnp.where(lane == 0, 0.0, pltpu.roll(vert, 1, 1))
@@ -123,11 +99,11 @@
             def load(j):
                 if j < 0 or j == rows:
                     side = 0 if j < 0 else 1
-                    ph = halo[side, 0, pl.ds(i0, CHUNK), :].astype(F32)
-                    co = halo[side, 1, pl.ds(i0, CHUNK), :].astype(F32)
+                    ph = halo[0, side, pl.ds(i0, CHUNK), :].astype(F32)
+                    co = halo[1, side, pl.ds(i0, CHUNK), :].astype(F32)
                 else:
-                    ph = row_of(ph_s, j, i0, CHUNK)
-                    co = row_of(co_s, j, i0, CHUNK)
+                    ph = phase[j, pl.ds(i0, CHUNK), :].astype(F32)
+                    co = coher[j, pl.ds(i0, CHUNK), :].astype(F32)
                 return ph * co, co
 
             window = [load(low - 1), load(low)]
@@ -177,29 +153,30 @@
     terrain_box = box_terrain(lambda h: h)
     square_box = box_terrain(lambda h: h * h)
 
+    if count < LANES:
+        mom[...] = jnp.zeros_like(mom)
+
     def moments(c, _):
-        start = pl.multiple_of(c * CHUNK * rows, CHUNK * rows)
-        top = jnp.zeros((CHUNK, rows, LANES), F32)
-        low = jnp.zeros((CHUNK, rows, LANES), F32)
-        for t in range(tiles):
-            cols = slice(t * LANES, (t + 1) * LANES)
-            co = co_s[t, pl.ds(start, CHUNK * rows), :].reshape(CHUNK, rows, LANES)
-            ph = ph_s[t, pl.ds(start, CHUNK * rows), :].reshape(CHUNK, rows, LANES)
-            top += co * ph * terrain_box[None, :, cols]
-            low += co * square_box[None, :, cols]
-        mom[0, pl.ds(start, CHUNK * rows), :] = top.reshape(CHUNK * rows, LANES)
-        mom[1, pl.ds(start, CHUNK * rows), :] = low.reshape(CHUNK * rows, LANES)
+        i0 = pl.multiple_of(c * CHUNK, CHUNK)
+        top = jnp.zeros((CHUNK, LANES), F32)
+        low = jnp.zeros((CHUNK, LANES), F32)
+        for j in range(rows):
+            co = coher[j, pl.ds(i0, CHUNK), :].astype(F32)
+            ph = phase[j, pl.ds(i0, CHUNK), :].astype(F32)
+            first = co * ph * terrain_box[j:j + 1, :]
+            second = co * square_box[j:j + 1, :]
+            for t in range(tiles):
+                cols = slice(t * LANES, (t + 1) * LANES)
+                top += first[:, cols]
+                low += second[:, cols]
+        mom[0, pl.ds(i0, CHUNK), :] = top
+        mom[1, pl.ds(i0, CHUNK), :] = low
         return 0
 
     lax.fori_loop(0, chunks, moments, 0)
 
     def summed(index):
-        total = mom[index, pl.ds(0, count, stride=rows), :]
-        for j in range(1, rows):
-            total += mom[index, pl.ds(j, count, stride=rows), :]
-        if count < LANES:
-            total = jnp.concatenate([total, jnp.zeros((LANES - count, LANES), F32)], axis=0)
-        return jnp.sum(total.T, axis=0, keepdims=True)
+        return jnp.sum(mom[index].T, axis=0, keepdims=True)
 
     mom_all[my_row] = jnp.concatenate([summed(0), summed(1), jnp.zeros((6, LANES), F32)], axis=0)
     mom_copies = []
@@ -208,8 +185,8 @@
         copy.start()
         mom_copies.append(copy)
 
-    lax.fori_loop(0, chunks, take_edges, 0)
-    edge_copies = start_pair(edge.at[0], edge.at[1], halo, halo_sems)
+    phase_copies = start_pair(phase.at[0], phase.at[rows - 1], halo.at[0], halo_sems.at[0])
+    coher_copies = start_pair(coher.at[0], coher.at[rows - 1], halo.at[1], halo_sems.at[1])
     for q in range(1, half - 1):
         smooth_rows(2 * q + 1, 2 * q + 3)
         w_copies.append(exchange(w_send, w_all, w_sems, q, 2 * q + 1, 2 * q + 3))
@@ -220,6 +197,17 @@
     gt[:, :ifgs] = signs[:DPAD].astype(BF16)
     gt[:, ifgs:] = signs[:DPAD].astype(BF16)
     g[...] = signs.T.astype(BF16)
+
+    pixel = lax.broadcasted_iota(jnp.int32, (rows * LANES, 2 * LANES), 0)
+    slot = lax.broadcasted_iota(jnp.int32, (rows * LANES, 2 * LANES), 1)
+    first_pixel = jnp.where(slot < rows, slot * LANES, -1)
+    last_pixel = jnp.where((slot >= LANES) & (slot < LANES + rows), (slot - LANES) * LANES + LANES - 1, -1)
+    pick[...] = ((pixel == first_pixel) | (pixel == last_pixel)).astype(F32).astype(BF16)
+    slot = lax.broadcasted_iota(jnp.int32, (2 * LANES, rows * LANES), 0)
+    pixel = lax.broadcasted_iota(jnp.int32, (2 * LANES, rows * LANES), 1)
+    first_pixel = jnp.where(slot < rows, slot * LANES, -1)
+    last_pixel = jnp.where((slot >= LANES) & (slot < LANES + rows), (slot - LANES) * LANES + LANES - 1, -1)
+    place[...] = ((pixel == first_pixel) | (pixel == last_pixel)).astype(F32).astype(BF16)
 
     for copy in mom_copies:
         copy.wait()
@@ -247,7 +235,8 @@
     for q in range(half - 1):
         correct_rows(2 * q + 1, 2 * q + 3)
         c_copies.append(exchange(c_send, c_all, c_sems, q, 2 * q + 1, 2 * q + 3))
-    wait_pair(edge_copies, halo)
+    wait_pair(phase_copies, halo.at[0])
+    wait_pair(coher_copies, halo.at[1])
     last = []
     for part, j in ((half - 1, rows - 1), (half, 0)):
         smooth_rows(j, j + 1)
@@ -280,16 +269,11 @@
     small = lax.broadcasted_iota(jnp.int32, (DPAD, LANES), 1)
 
     def start_halo(v, step):
-        first_packed = jnp.zeros((DPAD, LANES), F32)
-        last_packed = jnp.zeros((DPAD, LANES), F32)
-        for j in range(rows):
-            tile = v[j]
-            first_packed = jnp.where(small == j, pltpu.roll(tile, j, 1) if j else tile, first_packed)
-            last_packed = jnp.where(small == j, pltpu.roll(tile, j + 1, 1), last_packed)
         pack[step, 0] = v[0].astype(BF16)
         pack[step, 1] = v[rows - 1].astype(BF16)
-        pack[step, 2] = first_packed.astype(BF16)
-        pack[step, 3] = last_packed.astype(BF16)
+        packed = dot(jnp.concatenate([v[j].astype(BF16) for j in range(rows)], axis=1), pick[...])
+        pack[step, 2] = packed[:, :LANES].astype(BF16)
+        pack[step, 3] = packed[:, LANES:].astype(BF16)
         left, right = (lax.max(me - 1, 0), my_row), (lax.min(me + 1, n - 1), my_row)
         copies = (
             (has_up, remote(pack.at[step, 0], halo_row.at[step, 1], row_sems, (step, 0), up)),
@@ -326,16 +310,14 @@
             spread = 4.0 * here - around
             target[j] = target[j] + SMOOTHING_WEIGHT * spread + RIDGE_WEIGHT * here
         wait_halo(copies, step)
-        left_col, right_col = halo_col[step, 0].astype(F32), halo_col[step, 1].astype(F32)
+        beside = dot(jnp.concatenate([halo_col[step, 0], halo_col[step, 1]], axis=1), place[...])
         for j in range(rows):
-            left_edge = pltpu.roll(left_col, LANES - j, 1) if j else left_col
-            right_edge = pltpu.roll(right_col, LANES - 1 - j, 1)
-            beside = jnp.where(small == 0, left_edge, jnp.where(small == LANES - 1, right_edge, 0.0))
+            around = beside[:, j * LANES:(j + 1) * LANES]
             if j == 0:
-                beside += halo_row[step, 0].astype(F32)
+                around = around + halo_row[step, 0].astype(F32)
             if j == rows - 1:
-                beside += halo_row[step, 1].astype(F32)
-            target[j] = target[j] - SMOOTHING_WEIGHT * beside
+                around = around + halo_row[step, 1].astype(F32)
+            target[j] = target[j] - SMOOTHING_WEIGHT * around
 
     def apply(v, target, step, middle):
         copies = start_halo(v, step)
@@ -455,9 +437,7 @@
 
 
 def order_dates(x, topo, out, topo_out):
-    rows, dates, _ = x.shape
-    for j in range(rows):
-        out[pl.ds(j, dates, stride=rows), :] = x[j]
+    out[...] = jnp.swapaxes(x[...], 0, 1)
     topo_out[...] = topo[...]
 
 
@@ -467,7 +447,6 @@
     def per_device(phase, coherence, height, gap_mask, date_pairs):
         count, rows, width = phase.shape
         ifgs = date_pairs.shape[0]
-        tiles = width // LANES
         dma = pltpu.SemaphoreType.DMA
         state = pltpu.VMEM((rows, DPAD, LANES), F32)
         vmem = pl.BlockSpec(memory_space=pltpu.VMEM)
@@ -480,9 +459,6 @@
             in_specs=[vmem] * 5,
             out_specs=(vmem, vmem),
             scratch_shapes=[
-                pltpu.VMEM((tiles, count * rows, LANES), F32),
-                pltpu.VMEM((tiles, count * rows, LANES), F32),
-                pltpu.VMEM((2, 2, count, width), BF16),
                 pltpu.VMEM((2, 2, count, width), BF16),
                 pltpu.VMEM((rows, count, width), F32),
                 pltpu.VMEM((n, rows, count, LANES), BF16),
@@ -491,11 +467,13 @@
                 pltpu.VMEM((rows, ifgs, LANES), BF16),
                 pltpu.VMEM((2, rows, width), F32),
                 pltpu.VMEM((count, rows), F32),
-                pltpu.VMEM((2, count * rows, LANES), F32),
+                pltpu.VMEM((2, LANES, LANES), F32),
                 pltpu.VMEM((m, 8, LANES), F32),
                 pltpu.VMEM((LANES, LANES), F32),
                 pltpu.VMEM((ifgs, KPAD), BF16),
                 pltpu.VMEM((DPAD, 2 * ifgs), BF16),
+                pltpu.VMEM((rows * LANES, 2 * LANES), BF16),
+                pltpu.VMEM((2 * LANES, rows * LANES), BF16),
                 state, state, state, state, state, state,
                 pltpu.VMEM((3, 4, DPAD, LANES), BF16),
                 pltpu.VMEM((3, 2, DPAD, LANES), BF16),
@@ -503,7 +481,7 @@
                 pltpu.VMEM((3, n, 8, LANES), F32),
                 pltpu.VMEM((3, m, 8, LANES), F32),
                 dma((2, 2)),
-                dma((2, 2)),
+                dma((2, 2, 2)),
                 dma((2, rows // 2 + 1, n)),
                 dma((2, rows // 2 + 1, n)),
                 dma((2, m)),
@@ -515,12 +493,12 @@
             compiler_params=pltpu.CompilerParams(
                 collective_id=0, has_side_effects=True, vmem_limit_bytes=56 * 1024 * 1024
             ),
-        )(phase, coherence, height, gap_mask.T, date_pairs.T)
+        )(phase.transpose(1, 0, 2), coherence.transpose(1, 0, 2), height, gap_mask.T, date_pairs.T)
         displacement, topo = pl.pallas_call(
             order_dates,
             grid=(pl.cdiv(DATES, BLOCK),),
             out_shape=(
-                jax.ShapeDtypeStruct((DATES * rows, LANES), F32),
+                jax.ShapeDtypeStruct((DATES, rows, LANES), F32),
                 jax.ShapeDtypeStruct((1, count), F32),
             ),
             in_specs=[
@@ -528,11 +506,11 @@
                 pl.BlockSpec((1, count), lambda i: (0, 0)),
             ],
             out_specs=(
-                pl.BlockSpec((BLOCK * rows, LANES), lambda i: (i, 0)),
+                pl.BlockSpec((BLOCK, rows, LANES), lambda i: (i, 0, 0)),
                 pl.BlockSpec((1, count), lambda i: (0, 0)),
             ),
         )(field, topo)
-        return displacement.reshape(DATES, rows, LANES), topo.reshape(count)
+        return displacement, topo.reshape(count)
 
     return jax.shard_map(
         per_device,

time: 67.4 us -> 71.2 us (1.056)
  local copies, waits for them, and re-layouts: 0 us -> 3.57 us
    transpose x0 -> x1, local copies, waits for them, and re-layouts: none -> 3.57 us  [per_device(): coherence.transpose(1, 0, 2)]
where the time goes in v3:
time: 71.2 us; the launch traced here: 71 us
  Pallas kernels  66.7 us (94%)
  local copies, waits for them, and re-layouts  3.57 us (5%)
    pallas_call x1, Pallas kernels, per_device(): pl.pallas_call(functools.partial(kernel, n, m), out_shape=(jax.ShapeDtype...  63.5 us
    transpose x1, local copies, waits for them, and re-layouts, per_device(): coherence.transpose(1, 0, 2)  3.57 us
    pallas_call x1, Pallas kernels, per_device(): pl.pallas_call(order_dates, grid=(pl.cdiv(DATES, BLOCK),), out_shape=(jax...  3.27 us

profile of v3, /device:TPU:0, one launch (start us, length us, event | category | flops | bytes accessed | tf_op | source)
XLA Modules:
  0.0 71.0 jit_solution(7364488968833738113)
XLA Ops:
  0.6 3.6 %copy_bitcast_fusion = (bf16[8,128,512]{2,1,0:T(8,128)(2,1)}, bf16[8,128,512]{2,1,0:T(8,128)(2,1)}) fusion(bf16[128,8,512]{2,1,0:T(8,128)(2,1)} %param.6, bf16[128,8,512]{2,1,0:T(8,128)(2,1)} %param.5), kind=kLoop, calls=%fused_computation | loop fusion | bytes 4194304 | tf_op jit(solution)/shard_map/transpose | solution.py:496
  4.2 63.5 %shard_map.68 = (f32[8,304,128]{2,1,0:T(8,128)}, f32[1,128]{1,0:T(1,128)}) custom-call(bf16[8,128,512]{2,1,0:T(8,128)(2,1)} %get-tuple-element.11.phase, bf16[8,128,512]{2,1,0:T(8,128)(2,1)} %get-tuple-element.10.coher, f32[8,512]{1,0:T(8,128)} %height.1, s32[8,128]{1,0:T(8,128)} %bitcast.7, s32[2,512]{1,0:T(2,128)} %bitcast.8), custom_call_target="tpu_custom_call" | custom-call | tf_op jit(solution)/shard_map/pallas_call | solution.py:453
  67.7 3.3 %shard_map.69 = (f32[300,8,128]{2,1,0:T(8,128)}, f32[1,128]{1,0:T(1,128)}) custom-call(f32[8,304,128]{2,1,0:T(8,128)} %get-tuple-element.6.x, f32[1,128]{1,0:T(1,128)} %get-tuple-element.7.topo), custom_call_target="tpu_custom_call" | custom-call | tf_op jit(solution)/shard_map/pallas_call | solution.py:497

commit v4 on v2

--- a/solution.py
+++ b/solution.py
@@ -35,7 +35,7 @@
     phase, coher, height, gap, pairs,
     x_out, topo_out,
     ph_s, co_s, edge, halo, sm_s, w_send, w_all, c_send, c_all,
-    h_halo, gap_s, mom, mom_all, topo_s, g, gt,
+    h_halo, gap_s, mom, mom_all, topo_s, g, gt, pick, place,
     r_s, w_s, n_s, p_s, s_s, z_s,
     pack, halo_row, halo_col, red_a, red_b,
     h_sems, halo_sems, w_sems, c_sems, mom_sems, row_sems, col_sems, a_sems, b_sems,
@@ -221,6 +221,17 @@
     gt[:, ifgs:] = signs[:DPAD].astype(BF16)
     g[...] = signs.T.astype(BF16)
 
+    pixel = lax.broadcasted_iota(jnp.int32, (rows * LANES, 2 * LANES), 0)
+    slot = lax.broadcasted_iota(jnp.int32, (rows * LANES, 2 * LANES), 1)
+    first_pixel = jnp.where(slot < rows, slot * LANES, -1)
+    last_pixel = jnp.where((slot >= LANES) & (slot < LANES + rows), (slot - LANES) * LANES + LANES - 1, -1)
+    pick[...] = ((pixel == first_pixel) | (pixel == last_pixel)).astype(F32).astype(BF16)
+    slot = lax.broadcasted_iota(jnp.int32, (2 * LANES, rows * LANES), 0)
+    pixel = lax.broadcasted_iota(jnp.int32, (2 * LANES, rows * LANES), 1)
+    first_pixel = jnp.where(slot < rows, slot * LANES, -1)
+    last_pixel = jnp.where((slot >= LANES) & (slot < LANES + rows), (slot - LANES) * LANES + LANES - 1, -1)
+    place[...] = ((pixel == first_pixel) | (pixel == last_pixel)).astype(F32).astype(BF16)
+
     for copy in mom_copies:
         copy.wait()
     sums = mom_all[0]
@@ -280,16 +291,6 @@
     small = lax.broadcasted_iota(jnp.int32, (DPAD, LANES), 1)
 
     def start_halo(v, step):
-        first_packed = jnp.zeros((DPAD, LANES), F32)
-        last_packed = jnp.zeros((DPAD, LANES), F32)
-        for j in range(rows):
-            tile = v[j]
-            first_packed = jnp.where(small == j, pltpu.roll(tile, j, 1) if j else tile, first_packed)
-            last_packed = jnp.where(small == j, pltpu.roll(tile, j + 1, 1), last_packed)
-        pack[step, 0] = v[0].astype(BF16)
-        pack[step, 1] = v[rows - 1].astype(BF16)
-        pack[step, 2] = first_packed.astype(BF16)
-        pack[step, 3] = last_packed.astype(BF16)
         left, right = (lax.max(me - 1, 0), my_row), (lax.min(me + 1, n - 1), my_row)
         copies = (
             (has_up, remote(pack.at[step, 0], halo_row.at[step, 1], row_sems, (step, 0), up)),
@@ -297,7 +298,14 @@
             (has_left, remote(pack.at[step, 2], halo_col.at[step, 1], col_sems, (step, 0), left)),
             (has_right, remote(pack.at[step, 3], halo_col.at[step, 0], col_sems, (step, 1), right)),
         )
-        for there, copy in copies:
+        pack[step, 0] = v[0].astype(BF16)
+        pack[step, 1] = v[rows - 1].astype(BF16)
+        for there, copy in copies[:2]:
+            pl.when(there)(copy.start)
+        packed = dot(jnp.concatenate([v[j].astype(BF16) for j in range(rows)], axis=1), pick[...])
+        pack[step, 2] = packed[:, :LANES].astype(BF16)
+        pack[step, 3] = packed[:, LANES:].astype(BF16)
+        for there, copy in copies[2:]:
             pl.when(there)(copy.start)
         return copies
 
@@ -326,16 +334,14 @@
             spread = 4.0 * here - around
             target[j] = target[j] + SMOOTHING_WEIGHT * spread + RIDGE_WEIGHT * here
         wait_halo(copies, step)
-        left_col, right_col = halo_col[step, 0].astype(F32), halo_col[step, 1].astype(F32)
+        beside = dot(jnp.concatenate([halo_col[step, 0], halo_col[step, 1]], axis=1), place[...])
         for j in range(rows):
-            left_edge = pltpu.roll(left_col, LANES - j, 1) if j else left_col
-            right_edge = pltpu.roll(right_col, LANES - 1 - j, 1)
-            beside = jnp.where(small == 0, left_edge, jnp.where(small == LANES - 1, right_edge, 0.0))
+            around = beside[:, j * LANES:(j + 1) * LANES]
             if j == 0:
-                beside += halo_row[step, 0].astype(F32)
+                around = around + halo_row[step, 0].astype(F32)
             if j == rows - 1:
-                beside += halo_row[step, 1].astype(F32)
-            target[j] = target[j] - SMOOTHING_WEIGHT * beside
+                around = around + halo_row[step, 1].astype(F32)
+            target[j] = target[j] - SMOOTHING_WEIGHT * around
 
     def apply(v, target, step, middle):
         copies = start_halo(v, step)
@@ -350,34 +356,34 @@
 
     def reduce_first(step, parts):
         filled = list(parts) + [jnp.zeros((8 - len(parts), LANES), F32)]
-        red_a[step, me] = jnp.concatenate(filled, axis=0)
+        red_b[step, my_row] = jnp.concatenate(filled, axis=0)
         copies = []
+        for k in range(1, m):
+            copy = remote(red_b.at[step, my_row], red_b.at[step, my_row], b_sems, (step, k), (me, lax.rem(my_row + k, m)))
+            copy.start()
+            copies.append(copy)
+        return copies
+
+    def reduce_second(step, copies):
+        for copy in copies:
+            copy.wait()
+        total = red_b[step, 0]
+        for k in range(1, m):
+            total = total + red_b[step, k]
+        red_a[step, me] = total
+        later = []
         for k in range(1, n):
             copy = remote(red_a.at[step, me], red_a.at[step, me], a_sems, (step, k), (lax.rem(me + k, n), my_row))
             copy.start()
-            copies.append(copy)
-        return copies
-
-    def reduce_second(step, copies):
+            later.append(copy)
+        return later
+
+    def reduce_last(step, copies):
         for copy in copies:
             copy.wait()
         total = red_a[step, 0]
         for k in range(1, n):
             total = total + red_a[step, k]
-        red_b[step, my_row] = total
-        later = []
-        for k in range(1, m):
-            copy = remote(red_b.at[step, my_row], red_b.at[step, my_row], b_sems, (step, k), (me, lax.rem(my_row + k, m)))
-            copy.start()
-            later.append(copy)
-        return later
-
-    def reduce_last(step, copies):
-        for copy in copies:
-            copy.wait()
-        total = red_b[step, 0]
-        for k in range(1, m):
-            total = total + red_b[step, k]
         total = jnp.sum(total, axis=1, keepdims=True)
         return [total[i:i + 1, :] for i in range(3)]
 
@@ -496,6 +502,8 @@
                 pltpu.VMEM((LANES, LANES), F32),
                 pltpu.VMEM((ifgs, KPAD), BF16),
                 pltpu.VMEM((DPAD, 2 * ifgs), BF16),
+                pltpu.VMEM((rows * LANES, 2 * LANES), BF16),
+                pltpu.VMEM((2 * LANES, rows * LANES), BF16),
                 state, state, state, state, state, state,
                 pltpu.VMEM((3, 4, DPAD, LANES), BF16),
                 pltpu.VMEM((3, 2, DPAD, LANES), BF16),

time: 67.4 us -> 67.4 us (level)
  no operation moved by 1% of the time
where the time goes in v4:
time: 67.4 us; the launch traced here: 67.1 us
  Pallas kernels  66.5 us (99%)
    pallas_call x1, Pallas kernels, per_device(): pl.pallas_call(functools.partial(kernel, n, m), out_shape=(jax.ShapeDtype...  63.2 us
    pallas_call x1, Pallas kernels, per_device(): pl.pallas_call(order_dates, grid=(pl.cdiv(DATES, BLOCK),), out_shape=(jax...  3.32 us

profile of v4, /device:TPU:0, one launch (start us, length us, event | category | flops | bytes accessed | tf_op | source)
XLA Modules:
  0.0 67.1 jit_solution(14922046464069870434)
XLA Ops:
  0.6 63.2 %shard_map.68 = (f32[8,304,128]{2,1,0:T(8,128)}, f32[1,128]{1,0:T(1,128)}) custom-call(bf16[128,8,512]{2,1,0:T(8,128)(2,1)} %phase.1, bf16[128,8,512]{2,1,0:T(8,128)(2,1)} %coher.1, f32[8,512]{1,0:T(8,128)} %height.1, s32[8,128]{1,0:T(8,128)} %bitcast.4, s32[2,512]{1,0:T(2,128)} %bitcast.5), custom_call_target="tpu_custom_call" | custom-call | tf_op jit(solution)/shard_map/pallas_call | solution.py:480
  63.8 3.3 %shard_map.69 = (f32[2400,128]{1,0:T(8,128)}, f32[1,128]{1,0:T(1,128)}) custom-call(f32[8,304,128]{2,1,0:T(8,128)} %get-tuple-element.6.x, f32[1,128]{1,0:T(1,128)} %get-tuple-element.7.topo), custom_call_target="tpu_custom_call" | custom-call | tf_op jit(solution)/shard_map/pallas_call | solution.py:527

commit v5 on v4

--- a/solution.py
+++ b/solution.py
@@ -12,7 +12,7 @@
 KPAD = 640
 LANES = 128
 CHUNK = 16
-BLOCK = 104
+BLOCK = 304
 SMOOTHING_WEIGHT = 0.5
 RIDGE_WEIGHT = 0.05
 F32 = jnp.float32

time: 67.4 us -> 66.7 us (0.990)
  no operation moved by 1% of the time
where the time goes in v5:
time: 66.7 us; the launch traced here: 66.5 us
  Pallas kernels  65.9 us (99%)
    pallas_call x1, Pallas kernels, per_device(): pl.pallas_call(functools.partial(kernel, n, m), out_shape=(jax.ShapeDtype...  63.2 us
    pallas_call x1, Pallas kernels, per_device(): pl.pallas_call(order_dates, grid=(pl.cdiv(DATES, BLOCK),), out_shape=(jax...  2.68 us

profile of v5, /device:TPU:0, one launch (start us, length us, event | category | flops | bytes accessed | tf_op | source)
XLA Modules:
  0.0 66.5 jit_solution(3712311898725950708)
XLA Ops:
  0.6 63.2 %shard_map.68 = (f32[8,304,128]{2,1,0:T(8,128)}, f32[1,128]{1,0:T(1,128)}) custom-call(bf16[128,8,512]{2,1,0:T(8,128)(2,1)} %phase.1, bf16[128,8,512]{2,1,0:T(8,128)(2,1)} %coher.1, f32[8,512]{1,0:T(8,128)} %height.1, s32[8,128]{1,0:T(8,128)} %bitcast.4, s32[2,512]{1,0:T(2,128)} %bitcast.5), custom_call_target="tpu_custom_call" | custom-call | tf_op jit(solution)/shard_map/pallas_call | solution.py:480
  63.8 2.7 %shard_map.69 = (f32[2400,128]{1,0:T(8,128)}, f32[1,128]{1,0:T(1,128)}) custom-call(f32[8,304,128]{2,1,0:T(8,128)} %get-tuple-element.6.x, f32[1,128]{1,0:T(1,128)} %get-tuple-element.7.topo), custom_call_target="tpu_custom_call" | custom-call | tf_op jit(solution)/shard_map/pallas_call | solution.py:527
